TPU v7x, 256 devices: a whole 4x4x8 slice. The times are simulated.
256 devices in a mesh: ctx: 32 (over z, y_hi, core), exp: 8 (over y_lo, x).
Axes of the slice: x: 4, y: 4 (y_hi: 2, y_lo: 2; y = y_hi * 2 + y_lo), z: 8, core: 2. Of those that a mesh axis runs over, the one named last changes fastest.
Arguments:
- residual: bfloat16 [16384, 2048], P('ctx', 'exp'), may hold values from -6 to 6
- query_vectors: bfloat16 [16384, 2048], P('ctx', 'exp'), may hold values from -10 to 10
- key_vectors: bfloat16 [16384, 2048], P('ctx', 'exp'), may hold values from -10 to 10
- value_vectors: bfloat16 [16384, 2048], P('ctx', 'exp'), may hold values from -6 to 6
- out_weight: bfloat16 [2048, 2048], P('exp'), may hold values from -0.125 to 0.125
- norm_gain: float32 [2048], replicated, may hold values from 0.25 to 1.75
- species: int32 [2048, 1], P('ctx'), may hold values from 0 to 63; in each aligned block of 64 rows (0 to 63, 64 to 127, ...) at most 2 rows name the same one
- gate_weight: bfloat16 [64, 2048, 2816], P('ctx', None, 'exp'), may hold values from -0.125 to 0.125
- up_weight: bfloat16 [64, 2048, 2816], P('ctx', None, 'exp'), may hold values from -0.125 to 0.125
- down_weight: bfloat16 [64, 2816, 2048], P('ctx', 'exp'), may hold values from -0.109375 to 0.109375
Outputs:
- layer_out: bfloat16 [16384, 2048], P('ctx', 'exp')
Inputs may be any that keep to these rules, and one draw needn't show every extreme that they name: Among the 64 blocks of one device (aligned runs of rows of species) no species occurs more than 2 times; every species occurs somewhere.
All inputs are finite; a program needn't handle non-finite values.
Results may differ from a plain program's by a relative error of at most 0.02.
Values may be sent and summed in bfloat16 or wider, within the bound.
A program may use at most 128 MiB of HBM per device.

v0:
```python
import math

import jax
import jax.numpy as jnp
from jax import lax
from jax.sharding import PartitionSpec as P

HEAD_DIM = 128
BLK = 8
MOST = 2


EPSILON = 1e-06


def per_device(
    residual,
    query_vectors,
    key_vectors,
    value_vectors,
    out_weight,
    norm_gain,
    species,
    gate_weight,
    up_weight,
    down_weight,
):
    row_count = residual.shape[0]
    share_width = residual.shape[1]
    head_count = query_vectors.shape[1] // HEAD_DIM
    factor = 1.0 / math.sqrt(HEAD_DIM)
    query_heads = query_vectors.reshape(row_count, head_count, HEAD_DIM)
    initial = (
        jnp.full((head_count, row_count), -jnp.inf, jnp.float32),
        jnp.zeros((head_count, row_count), jnp.float32),
        jnp.zeros((head_count, row_count, HEAD_DIM), jnp.float32),
    )
    key_part = lax.all_gather(key_vectors, "ctx", axis=0, tiled=True)
    value_part = lax.all_gather(value_vectors, "ctx", axis=0, tiled=True)
    length = key_part.shape[0]
    block_len = math.gcd(length, 512)
    key_blocks = key_part.reshape(length // block_len, block_len, head_count, HEAD_DIM)
    value_blocks = value_part.reshape(length // block_len, block_len, head_count, HEAD_DIM)

    def advance(state_now, block_pair):
        running, denom_sum, weighted = state_now
        key_block, value_block = block_pair
        scores = (
            jnp.einsum("qhd,khd->hqk", query_heads, key_block, preferred_element_type=jnp.float32)
            * factor
        )
        new_running = jnp.maximum(running, jnp.max(scores, axis=-1))
        shrink = jnp.exp(running - new_running)
        weights = jnp.exp(scores - new_running[..., None])
        denom_sum = denom_sum * shrink + jnp.sum(weights, axis=-1)
        weighted = weighted * shrink[..., None] + jnp.einsum(
            "hqk,khd->hqd",
            weights.astype(jnp.bfloat16),
            value_block,
            preferred_element_type=jnp.float32,
        )
        return ((new_running, denom_sum, weighted), None)

    state_out, unused = lax.scan(advance, initial, (key_blocks, value_blocks))
    running, denom_sum, weighted = state_out
    attended = (
        (weighted / denom_sum[..., None])
        .transpose(1, 0, 2)
        .reshape(row_count, head_count * HEAD_DIM)
        .astype(jnp.bfloat16)
    )
    partial_value = jnp.dot(attended, out_weight, preferred_element_type=jnp.float32)
    stream_full = None
    stream_share = (
        residual.astype(jnp.float32)
        + lax.psum_scatter(
            partial_value.astype(jnp.bfloat16), "exp", scatter_dimension=1, tiled=True
        ).astype(jnp.float32)
    ).astype(jnp.bfloat16)
    expert_ids = species[:, 0]
    block_count = expert_ids.shape[0]
    local_experts = gate_weight.shape[0]
    ctx_count = lax.axis_size("ctx")
    slot_count = local_experts * ctx_count * MOST
    order = jnp.arange(block_count)
    earlier = (expert_ids[None, :] == expert_ids[:, None]) & (order[None, :] < order[:, None])
    slot_ids = expert_ids * MOST + jnp.sum(earlier, axis=1)
    selector = (jnp.arange(slot_count, dtype=jnp.int32)[:, None] == slot_ids[None, :]).astype(
        jnp.bfloat16
    )
    stream_full = lax.all_gather(stream_share, "exp", axis=1, tiled=True)
    full32 = stream_full.astype(jnp.float32)
    mean_sq = jnp.mean(full32 * full32, axis=1, keepdims=True)
    normed_full = (full32 * lax.rsqrt(mean_sq + EPSILON) * norm_gain).astype(jnp.bfloat16)
    columns = normed_full.shape[1]
    flat = normed_full.reshape(block_count, BLK * columns)
    packed = jnp.dot(selector, flat, preferred_element_type=jnp.float32).astype(jnp.bfloat16)
    arrived = lax.all_to_all(
        packed.reshape(ctx_count, local_experts, MOST * BLK, columns),
        "ctx",
        split_axis=0,
        concat_axis=0,
        tiled=True,
    )
    gate = jnp.einsum("sjrd,jdf->sjrf", arrived, gate_weight, preferred_element_type=jnp.float32)
    lifted = jnp.einsum("sjrd,jdf->sjrf", arrived, up_weight, preferred_element_type=jnp.float32)
    hidden = (jax.nn.silu(gate) * lifted).astype(jnp.bfloat16)
    parts = jnp.einsum("sjrf,jfd->sjrd", hidden, down_weight, preferred_element_type=jnp.float32)
    expert_out = lax.psum_scatter(
        parts.astype(jnp.bfloat16), "exp", scatter_dimension=3, tiled=True
    )
    returned = lax.all_to_all(expert_out, "ctx", split_axis=0, concat_axis=0, tiled=True)
    flat_back = returned.reshape(slot_count, BLK * share_width)
    moe_rows = jnp.einsum(
        "sb,sx->bx", selector, flat_back, preferred_element_type=jnp.float32
    ).reshape(row_count, share_width)
    return (stream_share.astype(jnp.float32) + moe_rows).astype(jnp.bfloat16)


def solution(mesh):
    return jax.shard_map(
        per_device,
        mesh=mesh,
        in_specs=(
            P("ctx", "exp"),
            P("ctx", "exp"),
            P("ctx", "exp"),
            P("ctx", "exp"),
            P("exp", None),
            P(),
            P("ctx", None),
            P("ctx", None, "exp"),
            P("ctx", None, "exp"),
            P("ctx", "exp", None),
        ),
        out_specs=P("ctx", "exp"),
        check_vma=False,
    )
```

profile of v0, /device:TPU:1, one launch (start us, length us, event | category | flops | bytes accessed | tf_op | source)
XLA Modules:
  0.0 826.0 jit_solution(8699130885730523486)
XLA Ops:
  9.4 106.5 %all-gather.4.cloned.1.call-done = bf16[16384,256]{1,0:T(8,128)(2,1)} async-done(((bf16[512,256]{1,0:T(8,128)(2,1)}), bf16[16384,256]{1,0:T(8,128)(2,1)}) %all-gather.4.cloned.1.call-update) | async-done | bytes 8388624 | tf_op jit(solution)/shard_map/all_gather | solution.py:38
  115.9 12.6 %reshape.54 = bf16[32,512,2,128]{3,2,1,0:T(2,128)(2,1)} reshape(bf16[16384,256]{1,0:T(8,128)(2,1)} %all-gather.4.cloned.1.call-done) | data formatting | bytes 16777216 | tf_op jit(solution)/shard_map/reshape | solution.py:42
  128.5 88.1 %all-gather.6.cloned.1.call-done = bf16[16384,256]{1,0:T(8,128)(2,1)} async-done(((bf16[512,256]{1,0:T(8,128)(2,1)}), bf16[16384,256]{1,0:T(8,128)(2,1)}) %all-gather.6.cloned.1.call-update) | async-done | bytes 8388624 | tf_op jit(solution)/shard_map/all_gather | solution.py:39
  216.6 12.5 %reshape.55 = bf16[32,512,2,128]{3,2,1,0:T(2,128)(2,1)} reshape(bf16[16384,256]{1,0:T(8,128)(2,1)} %all-gather.6.cloned.1.call-done) | data formatting | bytes 16777216 | tf_op jit(solution)/shard_map/reshape | solution.py:43
  229.1 266.9 %while.15 = (s32[]{:T(128)}, f32[2,512]{1,0:T(2,128)S(1)}, f32[2,512]{1,0:T(2,128)S(1)}, f32[2,512,128]{2,1,0:T(8,128)}, bf16[32,512,2,128]{3,2,1,0:T(2,128)(2,1...) while((s32[]{:T(128)}, f32[2,512]{1,0:T(2,128)S(1)}, ...), condition=%wide.region_3.4_spmd.clone, body=%wide.region_0.3_spmd.clone.sunk | while | flops 273028096 | bytes 9240685 | solution.py:64
  234.3 3.1 convolution_add_fusion.2
  242.6 3.2 convolution_add_fusion.2
  250.9 3.2 convolution_add_fusion.2
  259.2 3.2 convolution_add_fusion.2
  267.6 3.2 convolution_add_fusion.2
  275.9 3.2 convolution_add_fusion.2
  284.3 3.2 convolution_add_fusion.2
  292.6 3.2 convolution_add_fusion.2
  301.0 3.2 convolution_add_fusion.2
  309.3 3.2 convolution_add_fusion.2
  317.6 3.2 convolution_add_fusion.2
  326.0 3.2 convolution_add_fusion.2
  334.3 3.2 convolution_add_fusion.2
  342.7 3.2 convolution_add_fusion.2
  351.0 3.2 convolution_add_fusion.2
  359.4 3.2 convolution_add_fusion.2
  367.7 3.2 convolution_add_fusion.2
  376.0 3.2 convolution_add_fusion.2
  384.4 3.2 convolution_add_fusion.2
  392.7 3.2 convolution_add_fusion.2
  401.1 3.2 convolution_add_fusion.2
  409.4 3.2 convolution_add_fusion.2
  417.8 3.2 convolution_add_fusion.2
  426.1 3.2 convolution_add_fusion.2
  434.4 3.2 convolution_add_fusion.2
  442.8 3.2 convolution_add_fusion.2
  451.1 3.2 convolution_add_fusion.2
  459.5 3.2 convolution_add_fusion.2
  467.8 3.2 convolution_add_fusion.2
  476.1 3.2 convolution_add_fusion.2
  484.5 3.2 convolution_add_fusion.2
  492.8 3.2 convolution_add_fusion.2
  497.3 3.4 convolution_convert_fusion.1
  500.8 36.2 %reduce-scatter.3.cloned.1.call-done = bf16[512,256]{1,0:T(8,128)(2,1)} async-done(((bf16[512,2048]{1,0:T(8,128)(2,1)}), bf16[512,256]{1,0:T(8,128)(2,1)}) %reduce-scatter.3.cloned.1.call-update) | async-done | bytes 262160 | tf_op jit(solution)/shard_map/reduce_scatter | solution.py:76
  538.9 47.8 %all-gather.8.cloned.1.call-done = bf16[512,2048]{1,0:T(8,128)(2,1)} async-done(((bf16[512,256]{1,0:T(8,128)(2,1)}), bf16[512,2048]{1,0:T(8,128)(2,1)}) %all-gather.8.cloned.1.call-update) | async-done | bytes 2097168 | tf_op jit(solution)/shard_map/all_gather | solution.py:91
  590.9 4.2 reshape.47
  595.0 4.8 convolution_convert_fusion
  599.8 7.4 reshape.48
  607.3 109.5 %all_to_all.10 = bf16[32,2,16,2048]{3,2,1,0:T(8,128)(2,1)S(1)} all-to-all(bf16[32,2,16,2048]{3,2,1,0:T(8,128)(2,1)} %reshape.48), channel_id=1, replica_groups=mesh['ctx'=32,'exp'=8] {'ctx'}, dimensions={0} | all-to-all | bytes 8388608 | tf_op jit(solution)/shard_map/all_to_all | solution.py:98
  718.7 3.5 fusion.15
  722.3 8.3 %convert_bitcast_fusion = bf16[32,2,16,2048]{3,2,0,1:T(8,128)(2,1)} fusion(bf16[2,352,2048]{2,1,0:T(8,128)(2,1)S(1)} %copy-done, f32[2,32,16,352]{3,2,1,0:T(8,128)} %fusion.15, bf16[2,2048,352]{1,2,0:T(8,128)(2,1)} %param.20, bf16[32,2,16,2048]{3,2,1,0:T(8,128)(2,1)} %copy-done.2), kind=kOutput, calls=%fused_computation.26 | convolution fusion | flops 2957049856 | bytes 15597568 | tf_op jit(solution)/shard_map/sjrf,jfd->sjrd/dot_general | solution.py:108
  730.6 53.0 %reduce-scatter.5.cloned.1.call-done = bf16[32,2,16,256]{3,2,0,1:T(8,128)(2,1)} async-done(((bf16[32,2,16,2048]{3,2,0,1:T(8,128)(2,1)}), bf16[32,2,16,256]{3,2,0,1:T(8,128)(2,1)}) %reduce-scatter.5.cloned.1.call-update) | async-done | bytes 524304 | tf_op jit(solution)/shard_map/reduce_scatter | solution.py:109
  784.7 26.8 %all_to_all.11 = bf16[32,2,16,256]{3,2,1,0:T(8,128)(2,1)} all-to-all(bf16[32,2,16,256]{3,2,1,0:T(8,128)(2,1)S(1)} %copy.44), channel_id=1, replica_groups=mesh['ctx'=32,'exp'=8] {'ctx'}, dimensions={0} | all-to-all | bytes 1048576 | tf_op jit(solution)/shard_map/all_to_all | solution.py:112
  (236 shorter events, 186.0 us)
Async XLA Ops:
  6.5 715.7 %copy-start = (bf16[2,352,2048]{2,1,0:T(8,128)(2,1)S(1)}, bf16[2,352,2048]{2,1,0:T(8,128)(2,1)}, u32[]{:S(2)}) copy-start(bf16[2,352,2048]{2,1,0:T(8,128)(2,1)} %param.21) | copy-start | bytes 8650756
  6.5 109.3 %all-gather.4.cloned.1.call-start = ((), (), s32[]{:S(2)}) async-start(), calls=%async_computation.4 | async-start | bytes 8650752 | tf_op jit(solution)/shard_map/all_gather | solution.py:38
  7.3 209.4 %all-gather.6.cloned.1.call-start = ((), (), s32[]{:S(2)}) async-start(), calls=%async_computation.5 | async-start | bytes 8650752 | tf_op jit(solution)/shard_map/all_gather | solution.py:39
  8.0 528.9 %reduce-scatter.3.cloned.1.call-start = ((), (), s32[]{:S(2)}) async-start(), calls=%async_computation.6 | async-start | bytes 2359296 | tf_op jit(solution)/shard_map/reduce_scatter | solution.py:76
  497.3 39.6 %copy-start.4 = (bf16[512,256]{1,0:T(8,128)(2,1)S(1)}, bf16[512,256]{1,0:T(8,128)(2,1)}, u32[]{:S(2)}) copy-start(bf16[512,256]{1,0:T(8,128)(2,1)} %param.12) | copy-start | bytes 786436
  497.3 41.4 %copy-start.7 = (s32[64,1]{0,1:T(1,128)S(1)}, s32[64,1]{0,1:T(1,128)}, u32[]{:S(2)}) copy-start(s32[64,1]{0,1:T(1,128)} %param.18) | copy-start | bytes 772
  500.7 88.2 %copy-start.5 = (f32[2048]{0:T(1024)S(1)}, f32[2048]{0:T(1024)}, u32[]{:S(2)}) copy-start(f32[2048]{0:T(1024)} %param.17) | copy-start | bytes 24580
  500.7 86.0 %all-gather.8.cloned.1.call-start = ((), (), s32[]{:S(2)}) async-start(), calls=%async_computation.7 | async-start | bytes 2359296 | tf_op jit(solution)/shard_map/all_gather | solution.py:91
  538.7 244.9 %reduce-scatter.5.cloned.1.call-start = ((), (), s32[]{:S(2)}) async-start(), calls=%async_computation.8 | async-start | bytes 4718592 | tf_op jit(solution)/shard_map/reduce_scatter | solution.py:109
  586.7 2.2 copy-start.1
  607.3 111.5 %copy-start.6 = (bf16[2,2048,352]{1,2,0:T(8,128)(2,1)S(1)}, bf16[2,2048,352]{1,2,0:T(8,128)(2,1)}, u32[]{:S(2)}) copy-start(bf16[2,2048,352]{1,2,0:T(8,128)(2,1)} %param.19) | copy-start | bytes 8650756
  716.8 2.0 copy-start.2
  730.6 87.1 %copy-start.3 = (bf16[512,256]{1,0:T(8,128)(2,1)S(1)}, bf16[512,256]{1,0:T(8,128)(2,1)}, u32[]{:S(2)}) copy-start(bf16[512,256]{1,0:T(8,128)(2,1)} %add_convert_fusion.1) | copy-start | bytes 786436
Sparse Core Ops, SparseCore 0:
  10.1 105.6 all-gather.3
  118.6 97.9 all-gather.5
  500.9 36.0 reduce-scatter.2
  538.8 47.8 all-gather.7
  730.7 52.8 reduce-scatter.4
where the time goes:
time: 830 us; the launch traced here: 826 us
  waiting for transfers between devices  333 us (40%)
  matrix products  181 us (22%)
  blocking collectives  136 us (16%)
  local copies, waits for them, and re-layouts  90.9 us (11%)
  other arithmetic  71.2 us (9%)
  between operations  13.3 us (2%)
    all_to_all x1, blocking collectives, per_device(): lax.all_to_all(packed.reshape(ctx_count, local_experts, MOST * BLK, colum...  110 us
    all_gather x1, waiting for transfers between devices, per_device(): key_part = lax.all_gather(key_vectors, 'ctx', axis=0, tiled=True)  106 us
    dot_general x32, matrix products, advance(): jnp.einsum('hqk,khd->hqd', weights.astype(jnp.bfloat16), value_block, pre...  102 us
    all_gather x1, waiting for transfers between devices, per_device(): value_part = lax.all_gather(value_vectors, 'ctx', axis=0, tiled=True)  88.1 us
    reduce_sum x32, other arithmetic, advance(): denom_sum = denom_sum * shrink + jnp.sum(weights, axis=-1)  62.5 us
    dot_general x32, matrix products, advance(): jnp.einsum('qhd,khd->hqk', query_heads, key_block, preferred_element_type...  56.9 us
    reduce_scatter x1, waiting for transfers between devices, per_device(): lax.psum_scatter(parts.astype(jnp.bfloat16), 'exp', scatter_dimension=3,...  53 us
    all_gather x1, waiting for transfers between devices, per_device(): stream_full = lax.all_gather(stream_share, 'exp', axis=1, tiled=True)  47.8 us
  transfers between devices with their start and end apart: 5, of which 5 were waited for; matrix products, arithmetic and copies ran while one was open for 2% of the time, Pallas kernels for 0%

commit v1 on v0

v1 whole, which is shorter than its diff:
```python
import functools
import math

import jax
import jax.numpy as jnp
from jax import lax
from jax.experimental import pallas as pl
from jax.experimental.pallas import tpu as pltpu
from jax.sharding import PartitionSpec as P

HEAD_DIM = 128
BLK = 8
MOST = 2
EPSILON = 1e-06
EXP2_FACTOR = math.log2(math.e) / math.sqrt(HEAD_DIM)
VMEM_BYTES = 60 * 1024 * 1024
TILE_Q = 512
Z_CHUNKS = ((0, 1), (7, 2), (6, 3), (5, 4))
CHUNKS = len(Z_CHUNKS)
MESH = pl.DeviceIdType.MESH


def remote(src, dst, send_sem, recv_sem, where):
    return pltpu.make_async_remote_copy(
        src_ref=src,
        dst_ref=dst,
        send_sem=send_sem,
        recv_sem=recv_sem,
        device_id=where,
        device_id_type=MESH,
    )


def greet(others):
    barrier = pltpu.get_barrier_semaphore()
    for where in others:
        pl.semaphore_signal(barrier, inc=1, device_id=where, device_id_type=MESH)


def f32(value):
    return value.astype(jnp.float32)


def fused_kernel(
    q_ref, k_ref, v_ref, wo_ref, res_ref, gain_ref, ids_ref, gate_hbm, up_hbm, down_hbm,
    out_ref,
    qbuf, q_give, kv, kv_give, acc, top, o_send, att, wo_cols,
    gate, up, down, pack, unpack, stream, packed, agb, normed, back, fin,
    parts, ya, pp, hh, tt, yb,
    r_ss, r_rs, l_ss, l_rs, s_ss, s_rs, x_ss, x_rs, wo_ss, wo_rs, w_sem, a1_ss, a1_rs,
    rd_ss, rd_rs, ag_ss, ag_rs, b_ss, b_rs, f_ss, f_rs,
):
    ctx = lax.axis_index("ctx")
    z, lane = ctx // 4, ctx % 4
    exp = lax.axis_index("exp")
    x, y = exp % 4, exp // 4
    bf16 = jnp.bfloat16

    def at(dx, dy):
        return ((y + dy) % 2) * 4 + (x + dx) % 4

    def ctx_at(dz, dl):
        return ((z + dz) % 8) * 4 + (lane + dl) % 4

    me = at(0, 0)
    ahead, behind, across = {"exp": at(1, 0)}, {"exp": at(3, 0)}, {"exp": at(0, 1)}
    right, left = {"ctx": ctx_at(1, 0)}, {"ctx": ctx_at(7, 0)}
    sibling = {"ctx": z * 4 + (lane // 2) * 2 + (lane + 1) % 2}
    partner = {"ctx": ctx_at(0, 2)}

    exp_peers = [(dx, dy) for dy in range(2) for dx in range(4) if dx or dy]
    peers = [{"ctx": ctx_at(dz, dl)} for dz in range(8) for dl in range(4) if dz or dl]
    peers += [{"exp": at(dx, dy)} for dx, dy in exp_peers]
    greet(peers)
    loads = [
        pltpu.make_async_copy(src, dst, w_sem.at[i])
        for i, (src, dst) in enumerate(((gate_hbm, gate), (up_hbm, up), (down_hbm, down)))
    ]
    for load in loads:
        load.start()

    head, far_head = lane // 2, 1 - lane // 2
    mine = pl.ds(pl.multiple_of(head * HEAD_DIM, HEAD_DIM), HEAD_DIM)
    theirs = pl.ds(pl.multiple_of(far_head * HEAD_DIM, HEAD_DIM), HEAD_DIM)
    for place, cols in ((kv.at[0, 0, 0], mine), (kv_give, theirs)):
        for j in range(4):
            rows = slice(j * 128, (j + 1) * 128)
            place[0, j] = k_ref[rows, cols].T
            place[1, j] = v_ref[rows, cols]
    qbuf[0:512] = q_ref[:, mine]
    q_give[...] = q_ref[:, theirs]

    pl.semaphore_wait(pltpu.get_barrier_semaphore(), len(peers))

    def right_item(t):
        return 1 + t // 2, t % 2

    def left_item(t):
        return 7 - t // 2, t % 2 + t // 6

    def right_copy(t, p):
        slot, part = right_item(t)
        return remote(
            kv.at[0, slot - 1, part, p], kv.at[0, slot, part, p], r_ss.at[t, p], r_rs.at[t, p], right
        )

    def left_copy(t, p):
        slot, part = left_item(t)
        return remote(
            kv.at[0, (slot + 1) % 8, part, p],
            kv.at[0, slot, part, p],
            l_ss.at[t, p],
            l_rs.at[t, p],
            left,
        )

    def sibling_copy(way, t):
        slot, part = (right_item, left_item)[way](t)
        return remote(
            kv.at[0, slot, part], kv.at[1, slot, part], s_ss.at[way, t], s_rs.at[way, t], sibling
        )

    kv_copies = [
        remote(kv_give.at[p], kv.at[0, 0, 1, p], x_ss.at[p], x_rs.at[p], partner) for p in range(2)
    ]
    query_copy = remote(q_give, qbuf.at[pl.ds(512, 512)], x_ss.at[2], x_rs.at[2], partner)
    out_copy = remote(o_send, att.at[1, me], x_ss.at[3], x_rs.at[3], partner)
    near_copy = remote(kv.at[0, 0, 0], kv.at[1, 0, 0], x_ss.at[4], x_rs.at[4], sibling)
    far_copy = remote(kv.at[0, 0, 1], kv.at[1, 0, 1], x_ss.at[5], x_rs.at[5], sibling)
    for p in range(2):
        right_copy(0, p).start()
        left_copy(0, p).start()
        kv_copies[p].start()
    near_copy.start()
    query_copy.start()

    def wo_block(index):
        return pl.ds(pl.multiple_of(index * 256, 256), 256)

    def wo_copy(i):
        dx, dy = exp_peers[i]
        to = at(dx, dy)
        return remote(
            wo_ref.at[:, wo_block(to)], wo_cols.at[me], wo_ss.at[i], wo_rs.at[i], {"exp": to}
        )

    acc[...] = jnp.zeros_like(acc)
    top[...] = jnp.full_like(top, -1e30)
    ones = jnp.ones((512, HEAD_DIM), bf16)

    def attend(first, count, chunks):
        def one_tile(index, unused):
            rows = pl.ds(pl.multiple_of(first + index * TILE_Q, TILE_Q), TILE_Q)
            q = qbuf[rows, :]
            scores = [
                jnp.dot(
                    q,
                    jnp.concatenate([kv[kind, slot, part, 0, j] for j in range(4)], axis=1),
                    preferred_element_type=jnp.float32,
                )
                for kind, slot, part in chunks
            ]
            before = top[rows, :]
            best = functools.reduce(jnp.maximum, scores)
            best = jnp.maximum(best[:, :256], best[:, 256:])
            best = jnp.maximum(best[:, :128], best[:, 128:])
            now = jnp.maximum(before, jnp.max(best, axis=1, keepdims=True))
            top[rows, :] = now
            wide_now = jnp.concatenate([now] * 4, axis=1)
            total = None
            for s, (kind, slot, part) in zip(scores, chunks):
                weights = jnp.exp2((s - wide_now) * EXP2_FACTOR).astype(bf16)
                wide = jnp.concatenate([kv[kind, slot, part, 1].reshape(512, 128), ones], axis=1)
                term = jnp.dot(weights, wide, preferred_element_type=jnp.float32)
                total = term if total is None else total + term
            shrink = jnp.exp2((before - now) * EXP2_FACTOR)
            acc[rows, :] = acc[rows, :] * jnp.concatenate([shrink, shrink], axis=1) + total
            return unused

        lax.fori_loop(0, count // TILE_Q, one_tile, 0)

    attend(0, 512, [(0, 0, 0)])
    near_copy.wait_recv()
    attend(0, 512, [(1, 0, 0)])
    def counter(shape, dim):
        return lax.broadcasted_iota(jnp.int32, shape, dim)

    def flag(condition):
        return jnp.where(condition, 1.0, 0.0)

    ids = jnp.broadcast_to(f32(ids_ref[...]), (64, 64))
    ids_t = ids.T
    same = flag(ids == ids_t)
    before_row = flag(counter((64, 64), 0) < counter((64, 64), 1))
    before_col = flag(counter((64, 64), 1) < counter((64, 64), 0))
    slot_row = MOST * ids[0:1, :] + jnp.sum(same * before_row, axis=0, keepdims=True)
    slot_col = MOST * ids_t[:, 0:1] + jnp.sum(same * before_col, axis=1, keepdims=True)
    spans = flag(counter((64, 512), 1) // BLK == counter((64, 512), 0)).astype(bf16)
    spans_t = flag(counter((512, 64), 0) // BLK == counter((512, 64), 1)).astype(bf16)
    token_row = jnp.dot(
        jnp.broadcast_to(slot_row, (8, 64)).astype(bf16), spans, preferred_element_type=jnp.float32
    ).astype(jnp.int32)[0:1, :] * BLK + counter((1, 512), 1) % BLK
    token_col = jnp.dot(
        spans_t, jnp.broadcast_to(slot_col, (64, 128)).astype(bf16),
        preferred_element_type=jnp.float32,
    ).astype(jnp.int32) * BLK + counter((512, 128), 0) % BLK
    for part in range(4):
        places = counter((256, 512), 0) + part * 256
        pack[part * 256 : (part + 1) * 256, :] = flag(places == token_row).astype(bf16)
    for part in range(8):
        places = counter((512, 128), 1) + part * 128
        unpack[:, part * 128 : (part + 1) * 128] = flag(places == token_col).astype(bf16)
    for p in range(2):
        kv_copies[p].wait_recv()
        right_copy(1, p).start()
        left_copy(1, p).start()
    far_copy.start()
    attend(0, 512, [(0, 0, 1)])
    for i in range(7):
        wo_copy(i).start()
    wo_cols[me] = wo_ref[:, wo_block(me)]

    def pass_on(t):
        for p in range(2):
            right_copy(t, p).wait_recv()

            @pl.when(t < 5)
            def _():
                right_copy(t + 2, p).start()

            left_copy(t, p).wait_recv()

            @pl.when(t < 4)
            def _():
                left_copy(t + 2, p).start()

            @pl.when(t == 5)
            def _():
                left_copy(6, p).start()

        sibling_copy(0, t).start()
        sibling_copy(1, t).start()

    def stage(t, unused):
        pass_on(t)

        @pl.when(t == 0)
        def _():
            query_copy.wait_recv()
            far_copy.wait_recv()

        @pl.when(t < 5)
        def _():
            attend(512 * (1 - t // 4), 512, [(t % 2 + t // 4, 0, t // 2 - t // 4)])

        attend(0, 1024, [(0,) + right_item(t), (0,) + left_item(t)])
        sibling_copy(0, t).wait_recv()
        sibling_copy(1, t).wait_recv()
        attend(0, 1024, [(1,) + right_item(t), (1,) + left_item(t)])
        return unused

    lax.fori_loop(0, 6, stage, 0)

    def spread_copy(c, i):
        low, high = pl.ds(0, 256), pl.ds(256, 256)
        src, where = (
            (att.at[c, me], across),
            (att.at[c, me], ahead),
            (att.at[c, me], behind),
            (att.at[c, at(0, 1)], ahead),
            (att.at[c, at(0, 1)], behind),
            (att.at[c, at(3, 0), low], ahead),
            (att.at[c, at(1, 0), high], behind),
            (att.at[c, at(2, 0)], across),
        )[i]
        return remote(src, src, a1_ss.at[c, i], a1_rs.at[c, i], where)

    def spread_landed(c, i):
        low, high = pl.ds(0, 256), pl.ds(256, 256)
        dst = (
            att.at[c, at(0, 1)],
            att.at[c, at(3, 0)],
            att.at[c, at(1, 0)],
            att.at[c, at(3, 1)],
            att.at[c, at(1, 1)],
            att.at[c, at(2, 0), low],
            att.at[c, at(2, 0), high],
            att.at[c, at(2, 1)],
        )[i]
        remote(dst, dst, a1_ss.at[c, i], a1_rs.at[c, i], across).wait_recv()

    pass_on(6)
    attend(0, 512, [(0, 4, 0), (0, 4, 1)])
    sibling_copy(0, 6).wait_recv()
    sibling_copy(1, 6).wait_recv()
    attend(0, 512, [(1, 4, 0), (1, 4, 1)])
    att[0, me] = (acc[:512, :HEAD_DIM] / acc[:512, HEAD_DIM:]).astype(bf16)
    for i in range(3):
        spread_copy(0, i).start()
    attend(512, 512, [(0, 4, 0), (0, 4, 1)])
    attend(512, 512, [(1, 4, 0), (1, 4, 1)])
    o_send[...] = (acc[512:, :HEAD_DIM] / acc[512:, HEAD_DIM:]).astype(bf16)
    out_copy.start()
    for c in range(2):
        if c == 1:
            out_copy.wait_recv()
            for i in range(3):
                spread_copy(1, i).start()
        for i, nexts in ((0, (3, 4)), (1, (5,)), (2, (6,))):
            spread_landed(c, i)
            for n in nexts:
                spread_copy(c, n).start()
    for c in range(2):
        spread_landed(c, 5)
        spread_landed(c, 6)
        spread_copy(c, 7).start()
    for i in range(7):
        dx, dy = exp_peers[i]
        dst = wo_cols.at[at(4 - dx, dy)]
        remote(dst, dst, wo_ss.at[i], wo_rs.at[i], across).wait_recv()
    for c in range(2):
        for i in (3, 4, 7):
            spread_landed(c, i)
    near_rows, far_rows = mine, theirs
    for part in range(2):
        rows = slice(part * 256, (part + 1) * 256)
        total = f32(res_ref[rows, :])
        for f in range(8):
            total = total + jnp.dot(
                jnp.concatenate([att[0, f, rows, :], att[1, f, rows, :]], axis=1),
                jnp.concatenate([wo_cols[f, near_rows, :], wo_cols[f, far_rows, :]], axis=0),
                preferred_element_type=jnp.float32,
            )
        stream[rows, :] = total.astype(bf16)

    slots = [
        [(dz, dl) for dz in pair for dl in range(4)] for pair in Z_CHUNKS
    ]

    def send_copy(c, i):
        dz, dl = slots[c][i]
        to = ctx_at(dz, dl)
        return remote(
            packed.at[to], agb.at[c, me, :, i], b_ss.at[c, i], b_rs.at[c, i], {"ctx": to}
        )

    def back_copy(c, i):
        dz, dl = slots[c][i]
        to = ctx_at(8 - dz, 4 - dl)
        return remote(
            fin.at[c, :, i], back.at[ctx], f_ss.at[c, i], f_rs.at[c, i], {"ctx": to}
        )

    def remote_slots(c):
        return [i for i in range(8) if slots[c][i] != (0, 0)]

    for part in range(4):
        packed[part * 8 : (part + 1) * 8] = jnp.dot(
            pack[part * 256 : (part + 1) * 256, :], stream[...],
            preferred_element_type=jnp.float32,
        ).astype(jnp.bfloat16).reshape(8, 2, 16, 256)
    for c in range(CHUNKS):
        for i in remote_slots(c):
            send_copy(c, i).start()
    agb[0, me, :, 0] = packed[ctx]

    def gather_copy(c, i):
        src, where = (
            (agb.at[c, me], across),
            (agb.at[c, me], ahead),
            (agb.at[c, me], behind),
            (agb.at[c, at(0, 1)], ahead),
            (agb.at[c, at(0, 1)], behind),
            (agb.at[c, at(3, 0), 0], ahead),
            (agb.at[c, at(1, 0), 1], behind),
            (agb.at[c, at(2, 0)], across),
        )[i]
        return remote(src, src, ag_ss.at[c, i], ag_rs.at[c, i], where)

    def gather_first(c):
        for i in remote_slots(c):
            send_copy(c, i).wait_recv()
        for i in range(3):
            gather_copy(c, i).start()

    def landed(c, i):
        dst = (
            agb.at[c, at(0, 1)],
            agb.at[c, at(3, 0)],
            agb.at[c, at(1, 0)],
            agb.at[c, at(3, 1)],
            agb.at[c, at(1, 1)],
            agb.at[c, at(2, 0), 0],
            agb.at[c, at(2, 0), 1],
            agb.at[c, at(2, 1)],
        )[i]
        remote(dst, dst, ag_ss.at[c, i], ag_rs.at[c, i], across).wait_recv()

    def gather_second(c):
        landed(c, 0)
        gather_copy(c, 3).start()
        gather_copy(c, 4).start()
        landed(c, 1)
        gather_copy(c, 5).start()
        landed(c, 2)
        gather_copy(c, 6).start()

    def gather_third(c):
        landed(c, 5)
        landed(c, 6)
        gather_copy(c, 7).start()

    def gather_last(c):
        for i in (3, 4, 7):
            landed(c, i)

    half = 128
    low_rows, high_rows = pl.ds(0, half), pl.ds(half, half)

    def sum_copy(c, i):
        src, dst, where = (
            (parts.at[c, at(2, 1)], ya.at[c], across),
            (parts.at[c, at(1, 1)], pp.at[c, 0], ahead),
            (parts.at[c, at(3, 1)], pp.at[c, 1], behind),
            (parts.at[c, at(2, 0), low_rows], hh.at[c, 0], ahead),
            (parts.at[c, at(2, 0), high_rows], hh.at[c, 1], behind),
            (parts.at[c, at(1, 0)], tt.at[c, 0], ahead),
            (parts.at[c, at(3, 0)], tt.at[c, 1], behind),
            (parts.at[c, at(0, 1)], yb.at[c], across),
        )[i]
        return remote(src, dst, rd_ss.at[c, i], rd_rs.at[c, i], where)

    def sum_first(c):
        for i in range(3):
            sum_copy(c, i).start()

    def sum_second(c):
        sum_copy(c, 0).wait_recv()
        far = at(2, 0)
        parts[c, far] = (f32(parts[c, far]) + f32(ya[c])).astype(bf16)
        sum_copy(c, 3).start()
        sum_copy(c, 4).start()

    def sum_third(c):
        sum_copy(c, 1).wait_recv()
        sum_copy(c, 2).wait_recv()
        other = at(0, 1)
        parts[c, other] = (f32(parts[c, other]) + f32(pp[c, 0]) + f32(pp[c, 1])).astype(bf16)
        sum_copy(c, 7).start()
        for way, rows in ((0, low_rows), (1, high_rows)):
            sum_copy(c, 3 + way).wait_recv()
            near = at(1 if way == 0 else 3, 0)
            parts[c, near, rows] = (f32(parts[c, near, rows]) + f32(hh[c, way])).astype(bf16)
            sum_copy(c, 5 + way).start()

    def sum_last(c):
        for i in (5, 6, 7):
            sum_copy(c, i).wait_recv()
        return (f32(parts[c, me]) + f32(tt[c, 0])) + (f32(tt[c, 1]) + f32(yb[c]))

    def experts(c):
        square = jnp.zeros((256, 1), jnp.float32)
        for f in range(8):
            piece = f32(agb[c, f].reshape(256, 256))
            square = square + jnp.sum(piece * piece, axis=1, keepdims=True)
        scale = lax.rsqrt(square * (1.0 / 2048) + EPSILON)
        for f in range(8):
            cols = slice(f * 256, (f + 1) * 256)
            piece = f32(agb[c, f].reshape(256, 256))
            normed[:, cols] = (piece * scale * gain_ref[:, cols]).astype(jnp.bfloat16)
        for e in range(2):
            rows = slice(e * 128, (e + 1) * 128)
            lifted = lax.dot_general(
                normed[rows, :], up[e], (((1,), (1,)), ((), ())),
                preferred_element_type=jnp.float32,
            )
            gated = lax.dot_general(
                normed[rows, :], gate[e], (((1,), (1,)), ((), ())),
                preferred_element_type=jnp.float32,
            )
            hidden = (gated / (1.0 + jnp.exp(-gated)) * lifted).astype(jnp.bfloat16)
            for f in range(8):
                parts[c, f, rows, :] = jnp.dot(
                    hidden, down[e, :, f * 256 : (f + 1) * 256],
                    preferred_element_type=jnp.float32,
                ).astype(jnp.bfloat16)

    def finish(c):
        fin[c] = sum_last(c).astype(jnp.bfloat16).reshape(2, 8, 16, 256)
        for i in remote_slots(c):
            back_copy(c, i).start()
        if c == 0:
            back[ctx] = fin[0, :, 0]

    for step in range(CHUNKS):
        gather_first(step)
        if step >= 1:
            gather_second(step - 1)
        if step >= 2:
            gather_third(step - 2)
    for load in loads:
        load.wait()
    for step in range(CHUNKS + 3):
        if step == 0:
            gather_second(3)
            gather_third(2)
        if step == 1:
            gather_third(3)
        if step < CHUNKS:
            gather_last(step)
            experts(step)
            sum_first(step)
        if 0 <= step - 1 < CHUNKS:
            sum_second(step - 1)
        if 0 <= step - 2 < CHUNKS:
            sum_third(step - 2)
        if 0 <= step - 3 < CHUNKS:
            finish(step - 3)

    for c in range(CHUNKS):
        for i in remote_slots(c):
            dst = back.at[ctx_at(*slots[c][i])]
            remote(dst, dst, f_ss.at[c, i], f_rs.at[c, i], across).wait_recv()
    for rows in (slice(0, 256), slice(256, 512)):
        moved = jnp.dot(
            unpack[rows, :], back[...].reshape(1024, 256), preferred_element_type=jnp.float32
        )
        out_ref[rows, :] = (f32(stream[rows, :]) + moved).astype(jnp.bfloat16)

    def drain(t, unused):
        for p in range(2):
            right_copy(t, p).wait_send()
            left_copy(t, p).wait_send()
        sibling_copy(0, t).wait_send()
        sibling_copy(1, t).wait_send()
        return unused

    lax.fori_loop(0, 7, drain, 0)
    for copy in kv_copies + [query_copy, out_copy, near_copy, far_copy]:
        copy.wait_send()
    for i in range(7):
        wo_copy(i).wait_send()
    for c in range(2):
        for i in range(8):
            spread_copy(c, i).wait_send()
    for c in range(CHUNKS):
        for i in range(8):
            sum_copy(c, i).wait_send()
            gather_copy(c, i).wait_send()
        for i in remote_slots(c):
            send_copy(c, i).wait_send()
            back_copy(c, i).wait_send()


def layer(q, k, v, out_weight, residual, gain, ids, gate, up, down):
    rows, width = residual.shape
    dma = pltpu.SemaphoreType.DMA
    vmem, hbm = pl.BlockSpec(memory_space=pltpu.VMEM), pl.BlockSpec(memory_space=pl.ANY)
    bf16, single = jnp.bfloat16, jnp.float32
    pairs = [(7, 2), (7, 2), (2, 7), (6,), (7,)]
    sems = [dma(shape) for shape in pairs for _ in range(2)]
    return pl.pallas_call(
        fused_kernel,
        out_shape=jax.ShapeDtypeStruct((rows, width), bf16),
        in_specs=[vmem] * 7 + [hbm] * 3,
        out_specs=vmem,
        scratch_shapes=[
            pltpu.VMEM((1024, HEAD_DIM), bf16),
            pltpu.VMEM((512, HEAD_DIM), bf16),
            pltpu.VMEM((2, 8, 2, 2, 4, 128, 128), bf16),
            pltpu.VMEM((2, 4, 128, 128), bf16),
            pltpu.VMEM((1024, 2 * HEAD_DIM), single),
            pltpu.VMEM((1024, HEAD_DIM), single),
            pltpu.VMEM((512, HEAD_DIM), bf16),
            pltpu.VMEM((2, 8, 512, HEAD_DIM), bf16),
            pltpu.VMEM((8, 256, 256), bf16),
            pltpu.VMEM(gate.shape, bf16),
            pltpu.VMEM(up.shape, bf16),
            pltpu.VMEM(down.shape, bf16),
            pltpu.VMEM((1024, 512), bf16),
            pltpu.VMEM((512, 1024), bf16),
            pltpu.VMEM((512, 256), bf16),
            pltpu.VMEM((32, 2, 16, 256), bf16),
            pltpu.VMEM((CHUNKS, 8, 2, 8, 16, 256), bf16),
            pltpu.VMEM((256, 2048), bf16),
            pltpu.VMEM((32, 2, 16, 256), bf16),
            pltpu.VMEM((CHUNKS, 2, 8, 16, 256), bf16),
            pltpu.VMEM((CHUNKS, 8, 256, 256), bf16),
            pltpu.VMEM((CHUNKS, 256, 256), bf16),
            pltpu.VMEM((CHUNKS, 2, 256, 256), bf16),
            pltpu.VMEM((CHUNKS, 2, 128, 256), bf16),
            pltpu.VMEM((CHUNKS, 2, 256, 256), bf16),
            pltpu.VMEM((CHUNKS, 256, 256), bf16),
        ]
        + sems
        + [dma((3,)), dma((2, 8)), dma((2, 8))]
        + [dma((CHUNKS, 8)) for _ in range(8)],
        compiler_params=pltpu.CompilerParams(
            collective_id=0, has_side_effects=True, vmem_limit_bytes=VMEM_BYTES
        ),
        cost_estimate=pl.CostEstimate(
            flops=15 * 10**9, bytes_accessed=10**7, transcendentals=512 * 16384 * 2
        ),
    )(q, k, v, out_weight, residual, gain, ids, gate, up, down)


def per_device(
    residual,
    query_vectors,
    key_vectors,
    value_vectors,
    out_weight,
    norm_gain,
    species,
    gate_weight,
    up_weight,
    down_weight,
):
    return layer(
        query_vectors, key_vectors, value_vectors, out_weight, residual, norm_gain.reshape(1, -1),
        species.reshape(1, -1), jnp.swapaxes(gate_weight, 1, 2), jnp.swapaxes(up_weight, 1, 2), down_weight,
    )


def solution(mesh):
    return jax.shard_map(
        per_device,
        mesh=mesh,
        in_specs=(
            P("ctx", "exp"),
            P("ctx", "exp"),
            P("ctx", "exp"),
            P("ctx", "exp"),
            P("exp", None),
            P(),
            P("ctx", None),
            P("ctx", None, "exp"),
            P("ctx", None, "exp"),
            P("ctx", "exp", None),
        ),
        out_specs=P("ctx", "exp"),
        check_vma=False,
    )
```

time: 830 us -> 173 us (0.21)
  waiting for transfers between devices: 333 us -> 0 us
  matrix products: 181 us -> 0 us
  Pallas kernels: 0 us -> 171 us
  blocking collectives: 136 us -> 0 us
  local copies, waits for them, and re-layouts: 90.9 us -> 1.67 us
  other arithmetic: 71.2 us -> 0 us
  between operations: 13.3 us -> 0.01 us
    all_gather x3 -> x0, waiting for transfers between devices: 242 us -> none  [the longest x1 106 us: per_device(): key_part = lax.all_gather(key_vectors, 'ctx', axis=0, tiled=True)]
    dot_general x69 -> x0, matrix products: 181 us -> none  [the longest x32 102 us: advance(): jnp.einsum('hqk,khd->hqd', weights.astype(jnp.bfloat16), value_block, pre...]
    pallas_call x0 -> x1, Pallas kernels: none -> 171 us  [layer(): pl.pallas_call(fused_kernel, out_shape=jax.ShapeDtypeStruct((rows, width)...]
    all_to_all x2 -> x0, blocking collectives: 136 us -> none  [the longest x1 110 us: per_device(): lax.all_to_all(packed.reshape(ctx_count, local_experts, MOST * BLK, colum...]
    reduce_scatter x2 -> x0, waiting for transfers between devices: 89.2 us -> none  [the longest x1 53 us: per_device(): lax.psum_scatter(parts.astype(jnp.bfloat16), 'exp', scatter_dimension=3,...]
    reduce_sum x34 -> x0, other arithmetic: 64.8 us -> none  [the longest x32 62.5 us: advance(): denom_sum = denom_sum * shrink + jnp.sum(weights, axis=-1)]
    dynamic_slice x32 -> x0, local copies, waits for them, and re-layouts: 44.5 us -> none  [per_device(): state_out, unused = lax.scan(advance, initial, (key_blocks, value_blocks))]
    reshape x6 -> x0, local copies, waits for them, and re-layouts: 40.8 us -> none  [the longest x1 12.6 us: per_device(): key_part.reshape(length // block_len, block_len, head_count, HEAD_DIM)]
  transfers between devices with their start and end apart: 5 -> 0, of which waited for: 5 -> 0; matrix products, arithmetic and copies ran while one was open for 2% -> 0% of each run, Pallas kernels for 0% -> 0%
where the time goes in v1:
time: 173 us
  Pallas kernels  171 us (99%)
    pallas_call x1, Pallas kernels, layer(): pl.pallas_call(fused_kernel, out_shape=jax.ShapeDtypeStruct((rows, width)...  171 us

profile of v1, /device:TPU:1, one launch (start us, length us, event | category | flops | bytes accessed | tf_op | source)
XLA Modules:
  0.0 172.6 jit_solution(5704172475221888398)
XLA Ops:
  0.0 170.9 %shard_map.100 = bf16[512,256]{1,0:T(8,128)(2,1)} custom-call(bf16[512,256]{1,0:T(8,128)(2,1)} %q_ref.1, bf16[512,256]{1,0:T(8,128)(2,1)} %k_ref.1, bf16[512,256]{1,0:T(8,128)(2,1)} %v_ref.1, bf16[256,2048]{1,0:T(8,128)(2,1)} %wo_ref.1, bf16[512,256]{1,0:T(8,128)(2,1)} %res_ref.1, f32[1,2048]{1,0:T(1,128)} %bitcast.6, s32[1,64]{1,0:T(1,128)} %bitcast.7, ...), custom_call_target="tpu_custom_call" | custom-call | flops 15000000512 | bytes 10000000 | tf_op jit(solution)/shard_map/pallas_call | solution.py:562
  170.9 1.7 copy.12

commit v2 on v1

--- a/solution.py
+++ b/solution.py
@@ -15,8 +15,16 @@
 EXP2_FACTOR = math.log2(math.e) / math.sqrt(HEAD_DIM)
 VMEM_BYTES = 60 * 1024 * 1024
 TILE_Q = 512
-Z_CHUNKS = ((0, 1), (7, 2), (6, 3), (5, 4))
-CHUNKS = len(Z_CHUNKS)
+Z_ORDER = (0, 1, 7, 2, 6, 3, 5, 4)
+CHUNKS = ((0, 1), (1, 2), (2, 4), (4, 6), (6, 7), (7, 8))
+ORDER = (
+    (0, 0), (0, 1), (1, 0), (1, 1), (0, 2), (2, 0), (0, 3), (2, 1), (3, 0), (1, 2),
+    (4, 0), (0, 4), (0, 5), (1, 3), (3, 1), (5, 0), (4, 1), (2, 2), (5, 1), (1, 4),
+    (6, 0), (1, 5), (3, 2), (2, 3), (4, 2), (5, 2), (2, 4), (6, 1), (7, 0), (8, 0),
+    (3, 3), (4, 3), (5, 3), (2, 5), (7, 1), (6, 2), (3, 4), (8, 1), (4, 4), (5, 4),
+    (7, 2), (6, 3), (8, 2), (3, 5), (4, 5), (5, 5), (7, 3), (6, 4), (8, 3), (9, 0),
+    (9, 1), (7, 4), (6, 5), (7, 5), (9, 2), (8, 4), (9, 3), (8, 5), (9, 4), (9, 5),
+)
 MESH = pl.DeviceIdType.MESH
 
 
@@ -46,7 +54,7 @@
     out_ref,
     qbuf, q_give, kv, kv_give, acc, top, o_send, att, wo_cols,
     gate, up, down, pack, unpack, stream, packed, agb, normed, back, fin,
-    parts, ya, pp, hh, tt, yb,
+    parts, ya, pp, hh, tt, yb, yc,
     r_ss, r_rs, l_ss, l_rs, s_ss, s_rs, x_ss, x_rs, wo_ss, wo_rs, w_sem, a1_ss, a1_rs,
     rd_ss, rd_rs, ag_ss, ag_rs, b_ss, b_rs, f_ss, f_rs,
 ):
@@ -333,66 +341,75 @@
             )
         stream[rows, :] = total.astype(bf16)
 
-    slots = [
-        [(dz, dl) for dz in pair for dl in range(4)] for pair in Z_CHUNKS
-    ]
-
-    def send_copy(c, i):
-        dz, dl = slots[c][i]
-        to = ctx_at(dz, dl)
+    slots = [(n, dl) for n in range(8) for dl in range(4)]
+
+    def remote_slots(c):
+        return [s for s in slots if s[0] in range(*CHUNKS[c]) and s != (0, 0)]
+
+    def send_copy(n, dl):
+        to = ctx_at(Z_ORDER[n], dl)
         return remote(
-            packed.at[to], agb.at[c, me, :, i], b_ss.at[c, i], b_rs.at[c, i], {"ctx": to}
+            packed.at[to], agb.at[me, n, :, dl], b_ss.at[n, dl], b_rs.at[n, dl], {"ctx": to}
         )
 
-    def back_copy(c, i):
-        dz, dl = slots[c][i]
-        to = ctx_at(8 - dz, 4 - dl)
+    def back_copy(n, dl):
+        to = ctx_at(8 - Z_ORDER[n], 4 - dl)
         return remote(
-            fin.at[c, :, i], back.at[ctx], f_ss.at[c, i], f_rs.at[c, i], {"ctx": to}
+            fin.at[n, :, dl], back.at[ctx], f_ss.at[n, dl], f_rs.at[n, dl], {"ctx": to}
         )
-
-    def remote_slots(c):
-        return [i for i in range(8) if slots[c][i] != (0, 0)]
 
     for part in range(4):
         packed[part * 8 : (part + 1) * 8] = jnp.dot(
             pack[part * 256 : (part + 1) * 256, :], stream[...],
             preferred_element_type=jnp.float32,
-        ).astype(jnp.bfloat16).reshape(8, 2, 16, 256)
-    for c in range(CHUNKS):
-        for i in remote_slots(c):
-            send_copy(c, i).start()
-    agb[0, me, :, 0] = packed[ctx]
+        ).astype(bf16).reshape(8, 2, 16, 256)
+    for c in range(len(CHUNKS)):
+        for slot in remote_slots(c):
+            send_copy(*slot).start()
+    agb[me, 0, :, 0] = packed[ctx]
+
+    def span(c):
+        return pl.ds(CHUNKS[c][0], CHUNKS[c][1] - CHUNKS[c][0])
+
+    def some(c, way):
+        return pl.ds(1, 3) if c % 2 == way else pl.ds(0, 4)
+
+    def some_rows(c, way):
+        return pl.ds(16, 48) if c % 2 == way else pl.ds(0, 64)
 
     def gather_copy(c, i):
+        rows = span(c)
         src, where = (
-            (agb.at[c, me], across),
-            (agb.at[c, me], ahead),
-            (agb.at[c, me], behind),
-            (agb.at[c, at(0, 1)], ahead),
-            (agb.at[c, at(0, 1)], behind),
-            (agb.at[c, at(3, 0), 0], ahead),
-            (agb.at[c, at(1, 0), 1], behind),
-            (agb.at[c, at(2, 0)], across),
+            (agb.at[me, rows], across),
+            (agb.at[me, rows], ahead),
+            (agb.at[me, rows], behind),
+            (agb.at[at(0, 1), rows, :, some(c, 0)], ahead),
+            (agb.at[at(0, 1), rows, :, some(c, 1)], behind),
+            (agb.at[at(3, 0), rows, 0], ahead),
+            (agb.at[at(1, 0), rows, 1], behind),
+            (agb.at[at(2, 0), rows], across),
+            (agb.at[at(3 if c % 2 == 0 else 1, 0), rows, :, pl.ds(0, 1)], across),
         )[i]
         return remote(src, src, ag_ss.at[c, i], ag_rs.at[c, i], where)
 
     def gather_first(c):
-        for i in remote_slots(c):
-            send_copy(c, i).wait_recv()
+        for slot in remote_slots(c):
+            send_copy(*slot).wait_recv()
         for i in range(3):
             gather_copy(c, i).start()
 
     def landed(c, i):
+        rows = span(c)
         dst = (
-            agb.at[c, at(0, 1)],
-            agb.at[c, at(3, 0)],
-            agb.at[c, at(1, 0)],
-            agb.at[c, at(3, 1)],
-            agb.at[c, at(1, 1)],
-            agb.at[c, at(2, 0), 0],
-            agb.at[c, at(2, 0), 1],
-            agb.at[c, at(2, 1)],
+            agb.at[at(0, 1), rows],
+            agb.at[at(3, 0), rows],
+            agb.at[at(1, 0), rows],
+            agb.at[at(3, 1), rows, :, some(c, 0)],
+            agb.at[at(1, 1), rows, :, some(c, 1)],
+            agb.at[at(2, 0), rows, 0],
+            agb.at[at(2, 0), rows, 1],
+            agb.at[at(2, 1), rows],
+            agb.at[at(3 if c % 2 == 0 else 1, 1), rows, :, pl.ds(0, 1)],
         )[i]
         remote(dst, dst, ag_ss.at[c, i], ag_rs.at[c, i], across).wait_recv()
 
@@ -404,6 +421,7 @@
         gather_copy(c, 5).start()
         landed(c, 2)
         gather_copy(c, 6).start()
+        gather_copy(c, 8).start()
 
     def gather_third(c):
         landed(c, 5)
@@ -411,121 +429,127 @@
         gather_copy(c, 7).start()
 
     def gather_last(c):
-        for i in (3, 4, 7):
+        for i in (3, 4, 7, 8):
             landed(c, i)
 
-    half = 128
-    low_rows, high_rows = pl.ds(0, half), pl.ds(half, half)
-
     def sum_copy(c, i):
+        rows = span(c)
         src, dst, where = (
-            (parts.at[c, at(2, 1)], ya.at[c], across),
-            (parts.at[c, at(1, 1)], pp.at[c, 0], ahead),
-            (parts.at[c, at(3, 1)], pp.at[c, 1], behind),
-            (parts.at[c, at(2, 0), low_rows], hh.at[c, 0], ahead),
-            (parts.at[c, at(2, 0), high_rows], hh.at[c, 1], behind),
-            (parts.at[c, at(1, 0)], tt.at[c, 0], ahead),
-            (parts.at[c, at(3, 0)], tt.at[c, 1], behind),
-            (parts.at[c, at(0, 1)], yb.at[c], across),
+            (parts.at[at(2, 1), rows], ya.at[rows], across),
+            (parts.at[at(1, 1), rows, :, some_rows(c, 0)], pp.at[0, rows, :, some_rows(c, 0)], ahead),
+            (parts.at[at(3, 1), rows, :, some_rows(c, 1)], pp.at[1, rows, :, some_rows(c, 1)], behind),
+            (parts.at[at(2, 0), rows, 0], hh.at[0, rows], ahead),
+            (parts.at[at(2, 0), rows, 1], hh.at[1, rows], behind),
+            (parts.at[at(1, 0), rows], tt.at[0, rows], ahead),
+            (parts.at[at(3, 0), rows], tt.at[1, rows], behind),
+            (parts.at[at(0, 1), rows], yb.at[rows], across),
+            (parts.at[at(1 if c % 2 == 0 else 3, 1), rows, :, pl.ds(0, 16)], yc.at[rows], across),
         )[i]
         return remote(src, dst, rd_ss.at[c, i], rd_rs.at[c, i], where)
 
     def sum_first(c):
-        for i in range(3):
+        for i in (0, 1, 2, 8):
             sum_copy(c, i).start()
 
     def sum_second(c):
+        rows = span(c)
         sum_copy(c, 0).wait_recv()
         far = at(2, 0)
-        parts[c, far] = (f32(parts[c, far]) + f32(ya[c])).astype(bf16)
+        parts[far, rows] = (f32(parts[far, rows]) + f32(ya[rows])).astype(bf16)
         sum_copy(c, 3).start()
         sum_copy(c, 4).start()
 
     def sum_third(c):
+        rows = span(c)
         sum_copy(c, 1).wait_recv()
         sum_copy(c, 2).wait_recv()
-        other = at(0, 1)
-        parts[c, other] = (f32(parts[c, other]) + f32(pp[c, 0]) + f32(pp[c, 1])).astype(bf16)
+        other, short = at(0, 1), c % 2
+        few, most = pl.ds(0, 16), pl.ds(16, 48)
+        parts[other, rows, :, few] = (
+            f32(parts[other, rows, :, few]) + f32(pp[1 - short, rows, :, few])
+        ).astype(bf16)
+        parts[other, rows, :, most] = (
+            f32(parts[other, rows, :, most])
+            + f32(pp[0, rows, :, most])
+            + f32(pp[1, rows, :, most])
+        ).astype(bf16)
         sum_copy(c, 7).start()
-        for way, rows in ((0, low_rows), (1, high_rows)):
+
+    def sum_fourth(c):
+        rows, few = span(c), pl.ds(0, 16)
+        sum_copy(c, 8).wait_recv()
+        near = at(1 if c % 2 == 0 else 3, 0)
+        parts[near, rows, :, few] = (f32(parts[near, rows, :, few]) + f32(yc[rows])).astype(bf16)
+        for way in range(2):
             sum_copy(c, 3 + way).wait_recv()
             near = at(1 if way == 0 else 3, 0)
-            parts[c, near, rows] = (f32(parts[c, near, rows]) + f32(hh[c, way])).astype(bf16)
+            parts[near, rows, way] = (f32(parts[near, rows, way]) + f32(hh[way, rows])).astype(bf16)
             sum_copy(c, 5 + way).start()
 
     def sum_last(c):
+        rows = span(c)
         for i in (5, 6, 7):
             sum_copy(c, i).wait_recv()
-        return (f32(parts[c, me]) + f32(tt[c, 0])) + (f32(tt[c, 1]) + f32(yb[c]))
+        return (f32(parts[me, rows]) + f32(tt[0, rows])) + (f32(tt[1, rows]) + f32(yb[rows]))
 
     def experts(c):
-        square = jnp.zeros((256, 1), jnp.float32)
-        for f in range(8):
-            piece = f32(agb[c, f].reshape(256, 256))
-            square = square + jnp.sum(piece * piece, axis=1, keepdims=True)
-        scale = lax.rsqrt(square * (1.0 / 2048) + EPSILON)
-        for f in range(8):
-            cols = slice(f * 256, (f + 1) * 256)
-            piece = f32(agb[c, f].reshape(256, 256))
-            normed[:, cols] = (piece * scale * gain_ref[:, cols]).astype(jnp.bfloat16)
+        rows = span(c)
+        count = CHUNKS[c][1] - CHUNKS[c][0]
+        height = count * 64
         for e in range(2):
-            rows = slice(e * 128, (e + 1) * 128)
+            square = jnp.zeros((height, 1), jnp.float32)
+            for f in range(8):
+                piece = f32(agb[f, rows, e].reshape(height, 256))
+                square = square + jnp.sum(piece * piece, axis=1, keepdims=True)
+            scale = lax.rsqrt(square * (1.0 / 2048) + EPSILON)
+            for f in range(8):
+                cols = slice(f * 256, (f + 1) * 256)
+                piece = f32(agb[f, rows, e].reshape(height, 256))
+                normed[e, :height, cols] = (piece * scale * gain_ref[:, cols]).astype(bf16)
             lifted = lax.dot_general(
-                normed[rows, :], up[e], (((1,), (1,)), ((), ())),
+                normed[e, :height, :], up[e], (((1,), (1,)), ((), ())),
                 preferred_element_type=jnp.float32,
             )
             gated = lax.dot_general(
-                normed[rows, :], gate[e], (((1,), (1,)), ((), ())),
+                normed[e, :height, :], gate[e], (((1,), (1,)), ((), ())),
                 preferred_element_type=jnp.float32,
             )
-            hidden = (gated / (1.0 + jnp.exp(-gated)) * lifted).astype(jnp.bfloat16)
+            hidden = (gated / (1.0 + jnp.exp(-gated)) * lifted).astype(bf16)
             for f in range(8):
-                parts[c, f, rows, :] = jnp.dot(
+                parts[f, rows, e] = jnp.dot(
                     hidden, down[e, :, f * 256 : (f + 1) * 256],
                     preferred_element_type=jnp.float32,
-                ).astype(jnp.bfloat16)
+                ).astype(bf16).reshape(count, 64, 256)
 
     def finish(c):
-        fin[c] = sum_last(c).astype(jnp.bfloat16).reshape(2, 8, 16, 256)
-        for i in remote_slots(c):
-            back_copy(c, i).start()
+        rows = span(c)
+        count = CHUNKS[c][1] - CHUNKS[c][0]
+        fin[rows] = sum_last(c).astype(bf16).reshape(count, 2, 4, 16, 256)
+        for slot in remote_slots(c):
+            back_copy(*slot).start()
         if c == 0:
             back[ctx] = fin[0, :, 0]
 
-    for step in range(CHUNKS):
-        gather_first(step)
-        if step >= 1:
-            gather_second(step - 1)
-        if step >= 2:
-            gather_third(step - 2)
-    for load in loads:
-        load.wait()
-    for step in range(CHUNKS + 3):
-        if step == 0:
-            gather_second(3)
-            gather_third(2)
-        if step == 1:
-            gather_third(3)
-        if step < CHUNKS:
-            gather_last(step)
-            experts(step)
-            sum_first(step)
-        if 0 <= step - 1 < CHUNKS:
-            sum_second(step - 1)
-        if 0 <= step - 2 < CHUNKS:
-            sum_third(step - 2)
-        if 0 <= step - 3 < CHUNKS:
-            finish(step - 3)
-
-    for c in range(CHUNKS):
-        for i in remote_slots(c):
-            dst = back.at[ctx_at(*slots[c][i])]
-            remote(dst, dst, f_ss.at[c, i], f_rs.at[c, i], across).wait_recv()
+    steps = (
+        gather_first, gather_second, gather_third, gather_last, experts,
+        sum_first, sum_second, sum_third, sum_fourth, finish,
+    )
+    ready = False
+    for step, c in ORDER:
+        if steps[step] is experts and not ready:
+            for load in loads:
+                load.wait()
+            ready = True
+        steps[step](c)
+
+    for n, dl in slots[1:]:
+        dst = back.at[ctx_at(Z_ORDER[n], dl)]
+        remote(dst, dst, f_ss.at[n, dl], f_rs.at[n, dl], across).wait_recv()
     for rows in (slice(0, 256), slice(256, 512)):
         moved = jnp.dot(
             unpack[rows, :], back[...].reshape(1024, 256), preferred_element_type=jnp.float32
         )
-        out_ref[rows, :] = (f32(stream[rows, :]) + moved).astype(jnp.bfloat16)
+        out_ref[rows, :] = (f32(stream[rows, :]) + moved).astype(bf16)
 
     def drain(t, unused):
         for p in range(2):
@@ -543,13 +567,13 @@
     for c in range(2):
         for i in range(8):
             spread_copy(c, i).wait_send()
-    for c in range(CHUNKS):
-        for i in range(8):
+    for c in range(len(CHUNKS)):
+        for i in range(9):
             sum_copy(c, i).wait_send()
             gather_copy(c, i).wait_send()
-        for i in remote_slots(c):
-            send_copy(c, i).wait_send()
-            back_copy(c, i).wait_send()
+    for slot in slots[1:]:
+        send_copy(*slot).wait_send()
+        back_copy(*slot).wait_send()
 
 
 def layer(q, k, v, out_weight, residual, gain, ids, gate, up, down):
@@ -581,20 +605,22 @@
             pltpu.VMEM((512, 1024), bf16),
             pltpu.VMEM((512, 256), bf16),
             pltpu.VMEM((32, 2, 16, 256), bf16),
-            pltpu.VMEM((CHUNKS, 8, 2, 8, 16, 256), bf16),
-            pltpu.VMEM((256, 2048), bf16),
+            pltpu.VMEM((8, 8, 2, 4, 16, 256), bf16),
+            pltpu.VMEM((2, 128, 2048), bf16),
             pltpu.VMEM((32, 2, 16, 256), bf16),
-            pltpu.VMEM((CHUNKS, 2, 8, 16, 256), bf16),
-            pltpu.VMEM((CHUNKS, 8, 256, 256), bf16),
-            pltpu.VMEM((CHUNKS, 256, 256), bf16),
-            pltpu.VMEM((CHUNKS, 2, 256, 256), bf16),
-            pltpu.VMEM((CHUNKS, 2, 128, 256), bf16),
-            pltpu.VMEM((CHUNKS, 2, 256, 256), bf16),
-            pltpu.VMEM((CHUNKS, 256, 256), bf16),
+            pltpu.VMEM((8, 2, 4, 16, 256), bf16),
+            pltpu.VMEM((8, 8, 2, 64, 256), bf16),
+            pltpu.VMEM((8, 2, 64, 256), bf16),
+            pltpu.VMEM((2, 8, 2, 64, 256), bf16),
+            pltpu.VMEM((2, 8, 64, 256), bf16),
+            pltpu.VMEM((2, 8, 2, 64, 256), bf16),
+            pltpu.VMEM((8, 2, 64, 256), bf16),
+            pltpu.VMEM((8, 2, 16, 256), bf16),
         ]
         + sems
         + [dma((3,)), dma((2, 8)), dma((2, 8))]
-        + [dma((CHUNKS, 8)) for _ in range(8)],
+        + [dma((len(CHUNKS), 9)) for _ in range(4)]
+        + [dma((8, 4)) for _ in range(4)],
         compiler_params=pltpu.CompilerParams(
             collective_id=0, has_side_effects=True, vmem_limit_bytes=VMEM_BYTES
         ),

time: 173 us -> 167 us (0.965)
  Pallas kernels: 171 us -> 166 us
    pallas_call x1, Pallas kernels: 171 us -> 166 us  [layer(): pl.pallas_call(fused_kernel, out_shape=jax.ShapeDtypeStruct((rows, width)...]
where the time goes in v2:
time: 167 us
  Pallas kernels  166 us (99%)
  local copies, waits for them, and re-layouts  1.67 us (1%)
    pallas_call x1, Pallas kernels, layer(): pl.pallas_call(fused_kernel, out_shape=jax.ShapeDtypeStruct((rows, width)...  166 us

profile of v2, /device:TPU:1, one launch (start us, length us, event | category | flops | bytes accessed | tf_op | source)
XLA Modules:
  0.0 167.2 jit_solution(10210709896011172340)
XLA Ops:
  0.0 165.5 %shard_map.100 = bf16[512,256]{1,0:T(8,128)(2,1)} custom-call(bf16[512,256]{1,0:T(8,128)(2,1)} %q_ref.1, bf16[512,256]{1,0:T(8,128)(2,1)} %k_ref.1, bf16[512,256]{1,0:T(8,128)(2,1)} %v_ref.1, bf16[256,2048]{1,0:T(8,128)(2,1)} %wo_ref.1, bf16[512,256]{1,0:T(8,128)(2,1)} %res_ref.1, f32[1,2048]{1,0:T(1,128)} %bitcast.6, s32[1,64]{1,0:T(1,128)} %bitcast.7, ...), custom_call_target="tpu_custom_call" | custom-call | flops 15000000512 | bytes 10000000 | tf_op jit(solution)/shard_map/pallas_call | solution.py:586
  165.5 1.7 copy.12

commit v3 on v2

--- a/solution.py
+++ b/solution.py
@@ -18,12 +18,13 @@
 Z_ORDER = (0, 1, 7, 2, 6, 3, 5, 4)
 CHUNKS = ((0, 1), (1, 2), (2, 4), (4, 6), (6, 7), (7, 8))
 ORDER = (
-    (0, 0), (0, 1), (1, 0), (1, 1), (0, 2), (2, 0), (0, 3), (2, 1), (3, 0), (1, 2),
-    (4, 0), (0, 4), (0, 5), (1, 3), (3, 1), (5, 0), (4, 1), (2, 2), (5, 1), (1, 4),
-    (6, 0), (1, 5), (3, 2), (2, 3), (4, 2), (5, 2), (2, 4), (6, 1), (7, 0), (8, 0),
-    (3, 3), (4, 3), (5, 3), (2, 5), (7, 1), (6, 2), (3, 4), (8, 1), (4, 4), (5, 4),
-    (7, 2), (6, 3), (8, 2), (3, 5), (4, 5), (5, 5), (7, 3), (6, 4), (8, 3), (9, 0),
-    (9, 1), (7, 4), (6, 5), (7, 5), (9, 2), (8, 4), (9, 3), (8, 5), (9, 4), (9, 5),
+    (0, 0), (0, 1), (10, 0), (1, 0), (1, 1), (10, 1), (0, 2), (2, 0), (2, 1), (0, 3),
+    (1, 2), (0, 4), (3, 1), (3, 0), (0, 5), (1, 3), (4, 0), (10, 2), (10, 3), (2, 2),
+    (5, 0), (4, 1), (2, 3), (1, 4), (10, 4), (3, 2), (5, 1), (1, 5), (6, 0), (4, 2),
+    (10, 5), (5, 2), (3, 3), (4, 3), (6, 1), (2, 4), (7, 0), (5, 3), (2, 5), (8, 0),
+    (6, 2), (3, 4), (4, 4), (7, 1), (8, 1), (5, 4), (6, 3), (7, 2), (9, 0), (8, 2),
+    (3, 5), (4, 5), (6, 4), (5, 5), (7, 3), (8, 3), (7, 4), (9, 2), (9, 1), (6, 5),
+    (7, 5), (8, 4), (9, 3), (8, 5), (9, 4), (9, 5),
 )
 MESH = pl.DeviceIdType.MESH
 
@@ -269,17 +270,21 @@
 
     lax.fori_loop(0, 6, stage, 0)
 
+    def many(c, way):
+        return pl.ds(128, 384) if c == way else pl.ds(0, 512)
+
     def spread_copy(c, i):
         low, high = pl.ds(0, 256), pl.ds(256, 256)
         src, where = (
             (att.at[c, me], across),
             (att.at[c, me], ahead),
             (att.at[c, me], behind),
-            (att.at[c, at(0, 1)], ahead),
-            (att.at[c, at(0, 1)], behind),
+            (att.at[c, at(0, 1), many(c, 0)], ahead),
+            (att.at[c, at(0, 1), many(c, 1)], behind),
             (att.at[c, at(3, 0), low], ahead),
             (att.at[c, at(1, 0), high], behind),
             (att.at[c, at(2, 0)], across),
+            (att.at[c, at(3 if c == 0 else 1, 0), pl.ds(0, 128)], across),
         )[i]
         return remote(src, src, a1_ss.at[c, i], a1_rs.at[c, i], where)
 
@@ -289,11 +294,12 @@
             att.at[c, at(0, 1)],
             att.at[c, at(3, 0)],
             att.at[c, at(1, 0)],
-            att.at[c, at(3, 1)],
-            att.at[c, at(1, 1)],
+            att.at[c, at(3, 1), many(c, 0)],
+            att.at[c, at(1, 1), many(c, 1)],
             att.at[c, at(2, 0), low],
             att.at[c, at(2, 0), high],
             att.at[c, at(2, 1)],
+            att.at[c, at(3 if c == 0 else 1, 1), pl.ds(0, 128)],
         )[i]
         remote(dst, dst, a1_ss.at[c, i], a1_rs.at[c, i], across).wait_recv()
 
@@ -314,7 +320,7 @@
             out_copy.wait_recv()
             for i in range(3):
                 spread_copy(1, i).start()
-        for i, nexts in ((0, (3, 4)), (1, (5,)), (2, (6,))):
+        for i, nexts in ((1, (5,)), (2, (6, 8)), (0, (3, 4))):
             spread_landed(c, i)
             for n in nexts:
                 spread_copy(c, n).start()
@@ -327,7 +333,7 @@
         dst = wo_cols.at[at(4 - dx, dy)]
         remote(dst, dst, wo_ss.at[i], wo_rs.at[i], across).wait_recv()
     for c in range(2):
-        for i in (3, 4, 7):
+        for i in (3, 4, 7, 8):
             spread_landed(c, i)
     near_rows, far_rows = mine, theirs
     for part in range(2):
@@ -413,10 +419,12 @@
         )[i]
         remote(dst, dst, ag_ss.at[c, i], ag_rs.at[c, i], across).wait_recv()
 
-    def gather_second(c):
+    def gather_near(c):
         landed(c, 0)
         gather_copy(c, 3).start()
         gather_copy(c, 4).start()
+
+    def gather_second(c):
         landed(c, 1)
         gather_copy(c, 5).start()
         landed(c, 2)
@@ -532,7 +540,7 @@
 
     steps = (
         gather_first, gather_second, gather_third, gather_last, experts,
-        sum_first, sum_second, sum_third, sum_fourth, finish,
+        sum_first, sum_second, sum_third, sum_fourth, finish, gather_near,
     )
     ready = False
     for step, c in ORDER:
@@ -565,7 +573,7 @@
     for i in range(7):
         wo_copy(i).wait_send()
     for c in range(2):
-        for i in range(8):
+        for i in range(9):
             spread_copy(c, i).wait_send()
     for c in range(len(CHUNKS)):
         for i in range(9):
@@ -618,7 +626,7 @@
             pltpu.VMEM((8, 2, 16, 256), bf16),
         ]
         + sems
-        + [dma((3,)), dma((2, 8)), dma((2, 8))]
+        + [dma((3,)), dma((2, 9)), dma((2, 9))]
         + [dma((len(CHUNKS), 9)) for _ in range(4)]
         + [dma((8, 4)) for _ in range(4)],
         compiler_params=pltpu.CompilerParams(

time: 167 us -> 167 us (level)
  no operation moved by 1% of the time
where the time goes in v3:
time: 167 us
  Pallas kernels  165 us (99%)
  local copies, waits for them, and re-layouts  1.67 us (1%)
    pallas_call x1, Pallas kernels, layer(): pl.pallas_call(fused_kernel, out_shape=jax.ShapeDtypeStruct((rows, width)...  165 us

profile of v3, /device:TPU:1, one launch (start us, length us, event | category | flops | bytes accessed | tf_op | source)
XLA Modules:
  0.0 166.8 jit_solution(5627358545245609330)
XLA Ops:
  0.0 165.1 %shard_map.100 = bf16[512,256]{1,0:T(8,128)(2,1)} custom-call(bf16[512,256]{1,0:T(8,128)(2,1)} %q_ref.1, bf16[512,256]{1,0:T(8,128)(2,1)} %k_ref.1, bf16[512,256]{1,0:T(8,128)(2,1)} %v_ref.1, bf16[256,2048]{1,0:T(8,128)(2,1)} %wo_ref.1, bf16[512,256]{1,0:T(8,128)(2,1)} %res_ref.1, f32[1,2048]{1,0:T(1,128)} %bitcast.6, s32[1,64]{1,0:T(1,128)} %bitcast.7, ...), custom_call_target="tpu_custom_call" | custom-call | flops 15000000512 | bytes 10000000 | tf_op jit(solution)/shard_map/pallas_call | solution.py:594
  165.1 1.7 %copy.12 = bf16[512,256]{1,0:T(8,128)(2,1)} copy(bf16[512,256]{1,0:T(8,128)(2,1)} %shard_map.100) | data formatting | bytes 524288

commit v4 on v3

--- a/solution.py
+++ b/solution.py
@@ -16,15 +16,17 @@
 VMEM_BYTES = 60 * 1024 * 1024
 TILE_Q = 512
 Z_ORDER = (0, 1, 7, 2, 6, 3, 5, 4)
-CHUNKS = ((0, 1), (1, 2), (2, 4), (4, 6), (6, 7), (7, 8))
+CHUNKS = ((0, 1), (1, 2), (2, 3), (3, 4), (4, 5), (5, 6), (6, 7), (7, 8))
 ORDER = (
-    (0, 0), (0, 1), (10, 0), (1, 0), (1, 1), (10, 1), (0, 2), (2, 0), (2, 1), (0, 3),
-    (1, 2), (0, 4), (3, 1), (3, 0), (0, 5), (1, 3), (4, 0), (10, 2), (10, 3), (2, 2),
-    (5, 0), (4, 1), (2, 3), (1, 4), (10, 4), (3, 2), (5, 1), (1, 5), (6, 0), (4, 2),
-    (10, 5), (5, 2), (3, 3), (4, 3), (6, 1), (2, 4), (7, 0), (5, 3), (2, 5), (8, 0),
-    (6, 2), (3, 4), (4, 4), (7, 1), (8, 1), (5, 4), (6, 3), (7, 2), (9, 0), (8, 2),
-    (3, 5), (4, 5), (6, 4), (5, 5), (7, 3), (8, 3), (7, 4), (9, 2), (9, 1), (6, 5),
-    (7, 5), (8, 4), (9, 3), (8, 5), (9, 4), (9, 5),
+    (0, 0), (0, 1), (0, 2), (1, 0), (0, 3), (10, 0), (0, 4), (1, 2), (0, 5), (1, 1),
+    (1, 3), (10, 1), (2, 0), (0, 6), (10, 2), (1, 4), (2, 2), (10, 5), (3, 0), (1, 5),
+    (2, 1), (2, 3), (10, 3), (0, 7), (4, 0), (5, 0), (1, 6), (3, 2), (4, 2), (2, 4),
+    (3, 1), (3, 3), (10, 4), (2, 5), (5, 2), (6, 0), (4, 1), (5, 1), (4, 3), (10, 6),
+    (2, 6), (7, 0), (3, 4), (1, 7), (10, 7), (4, 4), (5, 3), (6, 2), (6, 1), (3, 5),
+    (4, 5), (2, 7), (8, 0), (5, 4), (3, 6), (5, 5), (7, 1), (6, 3), (4, 6), (8, 1),
+    (3, 7), (6, 4), (5, 6), (4, 7), (5, 7), (7, 3), (8, 3), (7, 2), (6, 5), (7, 4),
+    (7, 5), (9, 0), (8, 2), (6, 6), (9, 1), (8, 4), (9, 3), (6, 7), (8, 5), (7, 6),
+    (8, 6), (9, 2), (7, 7), (9, 4), (8, 7), (9, 5), (9, 6), (9, 7),
 )
 MESH = pl.DeviceIdType.MESH
 

time: 167 us -> 167 us (level)
  no operation moved by 1% of the time
where the time goes in v4:
time: 167 us
  Pallas kernels  165 us (99%)
  local copies, waits for them, and re-layouts  1.67 us (1%)
    pallas_call x1, Pallas kernels, layer(): pl.pallas_call(fused_kernel, out_shape=jax.ShapeDtypeStruct((rows, width)...  165 us

profile of v4, /device:TPU:1, one launch (start us, length us, event | category | flops | bytes accessed | tf_op | source)
XLA Modules:
  0.0 166.6 jit_solution(14668362253685466556)
XLA Ops:
  0.0 164.9 %shard_map.100 = bf16[512,256]{1,0:T(8,128)(2,1)} custom-call(bf16[512,256]{1,0:T(8,128)(2,1)} %q_ref.1, bf16[512,256]{1,0:T(8,128)(2,1)} %k_ref.1, bf16[512,256]{1,0:T(8,128)(2,1)} %v_ref.1, bf16[256,2048]{1,0:T(8,128)(2,1)} %wo_ref.1, bf16[512,256]{1,0:T(8,128)(2,1)} %res_ref.1, f32[1,2048]{1,0:T(1,128)} %bitcast.6, s32[1,64]{1,0:T(1,128)} %bitcast.7, ...), custom_call_target="tpu_custom_call" | custom-call | flops 15000000512 | bytes 10000000 | tf_op jit(solution)/shard_map/pallas_call | solution.py:596
  165.0 1.7 %copy.12 = bf16[512,256]{1,0:T(8,128)(2,1)} copy(bf16[512,256]{1,0:T(8,128)(2,1)} %shard_map.100) | data formatting | bytes 524288

commit v5 on v4

--- a/solution.py
+++ b/solution.py
@@ -53,9 +53,9 @@
 
 
 def fused_kernel(
-    q_ref, k_ref, v_ref, wo_ref, res_ref, gain_ref, ids_ref, gate_hbm, up_hbm, down_hbm,
+    q_ref, k_ref, v_ref, wo_hbm, res_hbm, gain_ref, ids_ref, gate_hbm, up_hbm, down_hbm,
     out_ref,
-    qbuf, q_give, kv, kv_give, acc, top, o_send, att, wo_cols,
+    wo_ref, res_ref, qbuf, q_give, kv, kv_give, acc, top, o_send, att, wo_cols,
     gate, up, down, pack, unpack, stream, packed, agb, normed, back, fin,
     parts, ya, pp, hh, tt, yb, yc,
     r_ss, r_rs, l_ss, l_rs, s_ss, s_rs, x_ss, x_rs, wo_ss, wo_rs, w_sem, a1_ss, a1_rs,
@@ -87,7 +87,11 @@
         pltpu.make_async_copy(src, dst, w_sem.at[i])
         for i, (src, dst) in enumerate(((gate_hbm, gate), (up_hbm, up), (down_hbm, down)))
     ]
-    for load in loads:
+    early = [
+        pltpu.make_async_copy(wo_hbm, wo_ref, w_sem.at[3]),
+        pltpu.make_async_copy(res_hbm, res_ref, w_sem.at[4]),
+    ]
+    for load in early + loads:
         load.start()
 
     head, far_head = lane // 2, 1 - lane // 2
@@ -227,6 +231,8 @@
         left_copy(1, p).start()
     far_copy.start()
     attend(0, 512, [(0, 0, 1)])
+    for load in early:
+        load.wait()
     for i in range(7):
         wo_copy(i).start()
     wo_cols[me] = wo_ref[:, wo_block(me)]
@@ -596,9 +602,11 @@
     return pl.pallas_call(
         fused_kernel,
         out_shape=jax.ShapeDtypeStruct((rows, width), bf16),
-        in_specs=[vmem] * 7 + [hbm] * 3,
+        in_specs=[vmem] * 3 + [hbm] * 2 + [vmem] * 2 + [hbm] * 3,
         out_specs=vmem,
         scratch_shapes=[
+            pltpu.VMEM(out_weight.shape, bf16),
+            pltpu.VMEM(residual.shape, bf16),
             pltpu.VMEM((1024, HEAD_DIM), bf16),
             pltpu.VMEM((512, HEAD_DIM), bf16),
             pltpu.VMEM((2, 8, 2, 2, 4, 128, 128), bf16),
@@ -628,7 +636,7 @@
             pltpu.VMEM((8, 2, 16, 256), bf16),
         ]
         + sems
-        + [dma((3,)), dma((2, 9)), dma((2, 9))]
+        + [dma((5,)), dma((2, 9)), dma((2, 9))]
         + [dma((len(CHUNKS), 9)) for _ in range(4)]
         + [dma((8, 4)) for _ in range(4)],
         compiler_params=pltpu.CompilerParams(

time: 167 us -> 167 us (level)
  no operation moved by 1% of the time
where the time goes in v5:
time: 167 us
  Pallas kernels  165 us (99%)
  local copies, waits for them, and re-layouts  1.67 us (1%)
    pallas_call x1, Pallas kernels, layer(): pl.pallas_call(fused_kernel, out_shape=jax.ShapeDtypeStruct((rows, width)...  165 us

profile of v5, /device:TPU:1, one launch (start us, length us, event | category | flops | bytes accessed | tf_op | source)
XLA Modules:
  0.0 166.5 jit_solution(12474506071552894840)
XLA Ops:
  0.0 164.9 %shard_map.100 = bf16[512,256]{1,0:T(8,128)(2,1)} custom-call(bf16[512,256]{1,0:T(8,128)(2,1)} %q_ref.1, bf16[512,256]{1,0:T(8,128)(2,1)} %k_ref.1, bf16[512,256]{1,0:T(8,128)(2,1)} %v_ref.1, bf16[256,2048]{1,0:T(8,128)(2,1)} %wo_hbm.1, bf16[512,256]{1,0:T(8,128)(2,1)} %res_hbm.1, f32[1,2048]{1,0:T(1,128)} %bitcast.6, s32[1,64]{1,0:T(1,128)} %bitcast.7, ...), custom_call_target="tpu_custom_call" | custom-call | flops 15000000512 | bytes 10000000 | tf_op jit(solution)/shard_map/pallas_call | solution.py:602
  164.9 1.7 %copy.12 = bf16[512,256]{1,0:T(8,128)(2,1)} copy(bf16[512,256]{1,0:T(8,128)(2,1)} %shard_map.100) | data formatting | bytes 524288
